TPU v7x, 32 devices: a whole 2x2x4 slice. The times are simulated.
32 devices in a mesh: ctx: 8 (over y, x, core), wa: 4 (over z).
Axes of the slice: x: 2, y: 2, z: 4, core: 2. Of those that a mesh axis runs over, the one named last changes fastest.
Arguments:
- tokens: bfloat16 [8, 1024, 768], P('wa', 'ctx'), may hold values from -6 to 6
- doc_lengths: int32 [8], replicated, may hold values from 256 to 1024, as said below
- group_deal: int32 [8, 8], replicated, may hold values from 0 to 7, each once within a row
- qkv_weight: bfloat16 [768, 2304], P('wa'), may hold values from -0.21875 to 0.21875
- out_weight: bfloat16 [768, 768], P('wa'), may hold values from -2.5 to 2.5
- up_weight: bfloat16 [768, 3072], P('wa'), may hold values from -0.21875 to 0.21875
- up_bias: bfloat16 [3072], P('wa'), may hold values from -3 to 3
- down_weight: bfloat16 [3072, 768], P('wa'), may hold values from -0.109375 to 0.109375
- proj_weight: bfloat16 [768, 128], P('wa'), may hold values from -0.21875 to 0.21875
- vectors: bfloat16 [8, 768], P(None, 'wa'), may hold values from -2 to 2
- cotangent: bfloat16 [8, 1024, 128], P('wa', 'ctx'), may hold values from -6 to 6
Outputs:
- embeddings: bfloat16 [8, 1024, 128], P('wa', 'ctx')
- tokens_grad: float32 [8, 1024, 768], P('wa', 'ctx')
- qkv_grad: float32 [768, 2304], P('wa')
- out_grad: float32 [768, 768], P('wa')
- up_grad: float32 [768, 3072], P('wa')
- bias_grad: float32 [3072], P('wa')
- down_grad: float32 [3072, 768], P('wa')
- proj_grad: float32 [768, 128], P('wa')
- vectors_grad: float32 [8, 768], P(None, 'wa')
Inputs may be any that keep to these rules, and one draw needn't show every extreme that they name: `doc_lengths`: every draw has a sequence with all 1024 slots valid. `group_deal`: each row is a permutation of the block numbers of a sequence.
All inputs are finite; a program needn't handle non-finite values.
Results may differ from a plain program's by a relative error of at most 0.023.
Values may be sent and summed in bfloat16 or wider, within the bound.
No kernel may reach another device: no remote copies, remote signals or barrier semaphores. Data moves between devices by JAX's collectives and lax.ppermute only.
A program may use at most 256 MiB of HBM per device.

v0:
```python
from functools import partial

import jax
import jax.numpy as jnp
from jax import lax
from jax.sharding import PartitionSpec as P

H = 12
HEAD = 64


NEG_FILL = -1e30
NORM_EPS = 1e-06
ROOT_HALF = 0.7071067811865476
DENSITY_SCALE = 0.3989422804014327


def norm_rows(inputs, gain_row, shift_row):
    middle = jnp.mean(inputs, axis=-1, keepdims=True)
    center = inputs - middle
    spread = jnp.mean(center * center, axis=-1, keepdims=True)
    scaled = lax.rsqrt(spread + NORM_EPS)
    unit_rows = center * scaled
    return (unit_rows * gain_row + shift_row, unit_rows, scaled)


def norm_back(grad_in, unit_rows, scaled, gain_row):
    gain_grad = jnp.sum(grad_in * unit_rows, axis=(0, 1))
    shift_grad = jnp.sum(grad_in, axis=(0, 1))
    inner_grad = grad_in * gain_row
    centered = inner_grad - jnp.mean(inner_grad, axis=-1, keepdims=True)
    result = scaled * (
        centered - unit_rows * jnp.mean(inner_grad * unit_rows, axis=-1, keepdims=True)
    )
    return (result, gain_grad, shift_grad)


def gelu_both(inner_sum):
    normal_cdf = 0.5 * (1.0 + lax.erf(inner_sum * ROOT_HALF))
    density = jnp.exp(-0.5 * inner_sum * inner_sum) * DENSITY_SCALE
    return (inner_sum * normal_cdf, normal_cdf + inner_sum * density)


def split_tiles(key_rows, value_rows, key_valid):
    key_count = key_rows.shape[0]
    tile_width = 512
    tile_count = key_count // tile_width
    return (
        key_rows.reshape(tile_count, tile_width, H, HEAD),
        value_rows.reshape(tile_count, tile_width, H, HEAD),
        key_valid.reshape(tile_count, tile_width),
    )


def masked_scores(queries, key_tile, mask_tile):
    products = jnp.einsum("qhd,khd->hqk", queries, key_tile, preferred_element_type=jnp.float32)
    return jnp.where(mask_tile[None, None, :], products, NEG_FILL)


def attend_forward(queries, key_rows, value_rows, key_valid):
    key_tiles, value_tiles, mask_tiles = split_tiles(key_rows, value_rows, key_valid)
    row_span = queries.shape[0]

    def stats_step(running, portion):
        highest, summed = running
        key_tile, mask_tile = portion
        scores = masked_scores(queries, key_tile, mask_tile)
        new_peak = jnp.maximum(highest, jnp.max(scores, axis=-1))
        raised = jnp.where(mask_tile[None, None, :], jnp.exp(scores - new_peak[:, :, None]), 0.0)
        return ((new_peak, summed * jnp.exp(highest - new_peak) + jnp.sum(raised, axis=-1)), None)

    start_peak = jnp.full((H, row_span), NEG_FILL, jnp.float32)
    start_sum = jnp.zeros((H, row_span), jnp.float32)
    (highest, summed), _ = lax.scan(stats_step, (start_peak, start_sum), (key_tiles, mask_tiles))
    logsum = highest + jnp.log(summed)

    def value_step(running, portion):
        key_tile, value_tile, mask_tile = portion
        scores = masked_scores(queries, key_tile, mask_tile)
        prob_low = jnp.where(
            mask_tile[None, None, :], jnp.exp(scores - logsum[:, :, None]), 0.0
        ).astype(jnp.bfloat16)
        return (
            running
            + jnp.einsum("hqk,khd->qhd", prob_low, value_tile, preferred_element_type=jnp.float32),
            None,
        )

    attended, _ = lax.scan(
        value_step,
        jnp.zeros((row_span, H, HEAD), jnp.float32),
        (key_tiles, value_tiles, mask_tiles),
    )
    return (attended, logsum)


def attend_backward(
    queries, key_rows, value_rows, key_valid, logsum, delta_rows, grad_heads, with_keys
):
    key_tiles, value_tiles, mask_tiles = split_tiles(key_rows, value_rows, key_valid)

    def back_step(running, portion):
        key_tile, value_tile, mask_tile = portion
        scores = masked_scores(queries, key_tile, mask_tile)
        prob_rows = jnp.where(mask_tile[None, None, :], jnp.exp(scores - logsum[:, :, None]), 0.0)
        prob_grad = jnp.einsum(
            "qhd,khd->hqk", grad_heads, value_tile, preferred_element_type=jnp.float32
        )
        score_low = (prob_rows * (prob_grad - delta_rows[:, :, None])).astype(jnp.bfloat16)
        running = running + jnp.einsum(
            "hqk,khd->qhd", score_low, key_tile, preferred_element_type=jnp.float32
        )
        value_part = jnp.einsum(
            "hqk,qhd->khd",
            prob_rows.astype(jnp.bfloat16),
            grad_heads,
            preferred_element_type=jnp.float32,
        )
        key_part = jnp.einsum(
            "hqk,qhd->khd", score_low, queries, preferred_element_type=jnp.float32
        )
        return (running, (key_part, value_part))

    start_grad = jnp.zeros(queries.shape, jnp.float32)
    query_grad, pieces = lax.scan(back_step, start_grad, (key_tiles, value_tiles, mask_tiles))
    key_count = key_rows.shape[0]
    return (
        query_grad,
        pieces[0].reshape(key_count, H * HEAD),
        pieces[1].reshape(key_count, H * HEAD),
    )


def body(
    tokens,
    doc_lengths,
    group_deal,
    qkv_weight,
    out_weight,
    up_weight,
    up_bias,
    down_weight,
    proj_weight,
    vectors,
    cotangent,
):
    gathered = (
        lax.all_gather(qkv_weight, "wa", axis=0, tiled=True),
        lax.all_gather(out_weight, "wa", axis=0, tiled=True),
        lax.all_gather(up_weight, "wa", axis=0, tiled=True),
        lax.all_gather(up_bias, "wa", axis=0, tiled=True),
        lax.all_gather(down_weight, "wa", axis=0, tiled=True),
        lax.all_gather(proj_weight, "wa", axis=0, tiled=True),
        lax.all_gather(vectors, "wa", axis=1, tiled=True),
    )
    qkv_full, out_full, up_full, bias_full, down_full, proj_full, vector_full = gathered
    seq_count, group_rows, model_width = tokens.shape
    ctx_count = lax.axis_size("ctx")
    seq_start = lax.axis_index("wa") * seq_count
    my_lengths = lax.dynamic_slice_in_dim(doc_lengths, seq_start, seq_count, 0)
    my_deal = lax.dynamic_slice_in_dim(group_deal, seq_start, seq_count, 0)
    offsets = jnp.tile(jnp.arange(group_rows, dtype=jnp.int32), ctx_count)
    positions = jnp.repeat(my_deal, group_rows, axis=1) * group_rows + offsets[None, :]
    key_valid = positions < my_lengths[:, None]
    query_valid = lax.dynamic_slice_in_dim(
        key_valid, lax.axis_index("ctx") * group_rows, group_rows, 1
    )
    row_mask = query_valid.astype(jnp.float32)[:, :, None]
    query_scale = HEAD ** (-0.5)
    mixed_rows = jnp.einsum("scd,de->sce", tokens, qkv_full, preferred_element_type=jnp.float32)
    queries = ((mixed_rows[:, :, :model_width] + vector_full[0]) * query_scale).astype(jnp.bfloat16)
    key_rows = mixed_rows[:, :, model_width : 2 * model_width].astype(jnp.bfloat16)
    value_rows = (mixed_rows[:, :, 2 * model_width :] + vector_full[1]).astype(jnp.bfloat16)
    all_keys, all_values = (
        lax.all_gather(key_rows, "ctx", axis=1, tiled=True),
        lax.all_gather(value_rows, "ctx", axis=1, tiled=True),
    )
    query_heads = queries.reshape(seq_count, group_rows, H, HEAD)
    attended, logsum = jax.vmap(attend_forward)(query_heads, all_keys, all_values, key_valid)
    attended_low = attended.reshape(seq_count, group_rows, model_width).astype(jnp.bfloat16)
    first_sum = tokens.astype(jnp.float32) + (
        jnp.einsum("scd,de->sce", attended_low, out_full, preferred_element_type=jnp.float32)
        + vector_full[2]
    )
    normed, unit_one, scale_one = norm_rows(first_sum, vector_full[3], vector_full[4])
    normed_low = normed.astype(jnp.bfloat16)
    inner_sum = (
        jnp.einsum("scd,df->scf", normed_low, up_full, preferred_element_type=jnp.float32)
        + bias_full
    )
    active, gelu_slope = gelu_both(inner_sum)
    active_low = active.astype(jnp.bfloat16)
    second_sum = normed + (
        jnp.einsum("scf,fd->scd", active_low, down_full, preferred_element_type=jnp.float32)
        + vector_full[5]
    )
    final_sum, unit_two, scale_two = norm_rows(second_sum, vector_full[6], vector_full[7])
    final_low = final_sum.astype(jnp.bfloat16)
    project = jnp.einsum("scd,de->sce", final_low, proj_full, preferred_element_type=jnp.float32)
    inverse = lax.rsqrt(jnp.sum(project * project, axis=-1, keepdims=True) + NORM_EPS)
    direction = project * inverse
    embeddings = (direction * row_mask).astype(jnp.bfloat16)
    upstream = cotangent.astype(jnp.float32) * row_mask
    project_grad = (
        inverse * (upstream - direction * jnp.sum(upstream * direction, axis=-1, keepdims=True))
    ).astype(jnp.bfloat16)
    proj_grad = jnp.einsum(
        "scd,sce->de", final_low, project_grad, preferred_element_type=jnp.float32
    )
    final_grad = jnp.einsum(
        "sce,de->scd", project_grad, proj_full, preferred_element_type=jnp.float32
    )
    second_grad, gain_two, shift_two = norm_back(final_grad, unit_two, scale_two, vector_full[6])
    down_low = second_grad.astype(jnp.bfloat16)
    down_grad = jnp.einsum("scf,scd->fd", active_low, down_low, preferred_element_type=jnp.float32)
    inner_grad = (
        jnp.einsum("scd,fd->scf", down_low, down_full, preferred_element_type=jnp.float32)
        * gelu_slope
    )
    bias_grad = jnp.sum(inner_grad, axis=(0, 1))
    inner_low = inner_grad.astype(jnp.bfloat16)
    up_grad = jnp.einsum("scd,scf->df", normed_low, inner_low, preferred_element_type=jnp.float32)
    normed_grad = second_grad + jnp.einsum(
        "scf,df->scd", inner_low, up_full, preferred_element_type=jnp.float32
    )
    first_grad, gain_one, shift_one = norm_back(normed_grad, unit_one, scale_one, vector_full[3])
    first_low = first_grad.astype(jnp.bfloat16)
    out_grad = jnp.einsum(
        "scd,sce->de", attended_low, first_low, preferred_element_type=jnp.float32
    )
    attended_grad = jnp.einsum(
        "sce,de->scd", first_low, out_full, preferred_element_type=jnp.float32
    ).astype(jnp.bfloat16)
    grad_heads = attended_grad.reshape(seq_count, group_rows, H, HEAD)
    delta_rows = jnp.sum(grad_heads.astype(jnp.float32) * attended, axis=-1)
    delta_heads = jnp.swapaxes(delta_rows, 1, 2)
    query_grad, key_terms, value_terms = jax.vmap(partial(attend_backward, with_keys=True))(
        query_heads, all_keys, all_values, key_valid, logsum, delta_heads, grad_heads
    )
    key_grad, value_grad = (
        lax.psum_scatter(
            key_terms.astype(jnp.bfloat16), "ctx", scatter_dimension=1, tiled=True
        ).astype(jnp.float32),
        lax.psum_scatter(
            value_terms.astype(jnp.bfloat16), "ctx", scatter_dimension=1, tiled=True
        ).astype(jnp.float32),
    )
    query_part = (
        query_grad.reshape(seq_count, group_rows, model_width).astype(jnp.bfloat16) * query_scale
    )
    value_part = value_grad.astype(jnp.bfloat16)
    mixed_grad = jnp.concatenate([query_part, key_grad.astype(jnp.bfloat16), value_part], axis=-1)
    qkv_grad = jnp.einsum("scd,sce->de", tokens, mixed_grad, preferred_element_type=jnp.float32)
    tokens_grad = first_grad + jnp.einsum(
        "sce,de->scd", mixed_grad, qkv_full, preferred_element_type=jnp.float32
    )
    vectors_grad = jnp.stack(
        [
            jnp.sum(query_part.astype(jnp.float32), axis=(0, 1)),
            jnp.sum(value_part.astype(jnp.float32), axis=(0, 1)),
            jnp.sum(first_grad, axis=(0, 1)),
            gain_one,
            shift_one,
            jnp.sum(second_grad, axis=(0, 1)),
            gain_two,
            shift_two,
        ],
        axis=0,
    )
    owned = (
        lax.psum_scatter(
            qkv_grad.astype(jnp.bfloat16), "wa", scatter_dimension=0, tiled=True
        ).astype(jnp.float32),
        lax.psum_scatter(
            out_grad.astype(jnp.bfloat16), "wa", scatter_dimension=0, tiled=True
        ).astype(jnp.float32),
        lax.psum_scatter(
            up_grad.astype(jnp.bfloat16), "wa", scatter_dimension=0, tiled=True
        ).astype(jnp.float32),
        lax.psum_scatter(
            bias_grad.astype(jnp.bfloat16), "wa", scatter_dimension=0, tiled=True
        ).astype(jnp.float32),
        lax.psum_scatter(
            down_grad.astype(jnp.bfloat16), "wa", scatter_dimension=0, tiled=True
        ).astype(jnp.float32),
        lax.psum_scatter(
            proj_grad.astype(jnp.bfloat16), "wa", scatter_dimension=0, tiled=True
        ).astype(jnp.float32),
        lax.psum_scatter(
            vectors_grad.astype(jnp.bfloat16), "wa", scatter_dimension=1, tiled=True
        ).astype(jnp.float32),
    )
    summed = (
        lax.psum(owned[0].astype(jnp.bfloat16), "ctx").astype(jnp.float32),
        lax.psum(owned[1].astype(jnp.bfloat16), "ctx").astype(jnp.float32),
        lax.psum(owned[2].astype(jnp.bfloat16), "ctx").astype(jnp.float32),
        lax.psum(owned[3].astype(jnp.bfloat16), "ctx").astype(jnp.float32),
        lax.psum(owned[4].astype(jnp.bfloat16), "ctx").astype(jnp.float32),
        lax.psum(owned[5].astype(jnp.bfloat16), "ctx").astype(jnp.float32),
        lax.psum(owned[6].astype(jnp.bfloat16), "ctx").astype(jnp.float32),
    )
    return (
        embeddings,
        tokens_grad,
        summed[0],
        summed[1],
        summed[2],
        summed[3],
        summed[4],
        summed[5],
        summed[6],
    )


def solution(mesh):
    in_specs = (
        P("wa", "ctx", None),
        P(),
        P(),
        P("wa", None),
        P("wa", None),
        P("wa", None),
        P("wa"),
        P("wa", None),
        P("wa", None),
        P(None, "wa"),
        P("wa", "ctx", None),
    )
    out_specs = (
        P("wa", "ctx", None),
        P("wa", "ctx", None),
        P("wa", None),
        P("wa", None),
        P("wa", None),
        P("wa"),
        P("wa", None),
        P("wa", None),
        P(None, "wa"),
    )
    return jax.shard_map(body, mesh=mesh, in_specs=in_specs, out_specs=out_specs, check_vma=False)
```

profile of v0, /device:TPU:8, one launch (start us, length us, event | category | flops | bytes accessed | tf_op | source)
XLA Modules:
  0.0 944.7 jit_solution(11446303625677070540)
XLA Ops:
  8.0 13.5 %all-gather = bf16[4,192,8]{1,2,0:T(8,128)(2,1)S(1)} all-gather(bf16[1,192,8]{1,2,0:T(8,128)(2,1)} %bitcast.249), channel_id=1, replica_groups=mesh['ctx'=8,'wa'=4] {'wa'}, dimensions={0}, use_global_device_ids=true | all-gather | bytes 15360 | tf_op jit(solution)/shard_map/all_gather | solution.py:154
  22.2 56.0 %all-gather.9.cloned.1.call-done = bf16[768,2304]{1,0:T(8,128)(2,1)} async-done(((bf16[192,2304]{1,0:T(8,128)(2,1)}), bf16[768,2304]{1,0:T(8,128)(2,1)}) %all-gather.9.cloned.1.call-update) | async-done | bytes 3538960 | tf_op jit(solution)/shard_map/all_gather | solution.py:148
  86.8 13.1 %all-gather.1 = bf16[4,1,768]{2,1,0:T(2,128)(2,1)S(1)} all-gather(bf16[1,1,768]{2,1,0:T(2,128)(2,1)S(1)} %reshape.193), channel_id=1, replica_groups=mesh['ctx'=8,'wa'=4] {'wa'}, dimensions={0}, use_global_device_ids=true | all-gather | bytes 7680 | tf_op jit(solution)/shard_map/all_gather | solution.py:151
  101.3 14.5 %all_gather.35 = bf16[768,128]{1,0:T(8,128)(2,1)} all-gather(bf16[192,128]{1,0:T(8,128)(2,1)S(1)} %copy-done.36), channel_id=1, replica_groups=mesh['ctx'=8,'wa'=4] {'wa'}, dimensions={0}, use_global_device_ids=true | all-gather | bytes 245760 | tf_op jit(solution)/shard_map/all_gather | solution.py:153
  128.3 22.5 %all-gather.13.cloned.1.call-done = bf16[2,1024,768]{2,1,0:T(8,128)(2,1)} async-done(((bf16[2,128,768]{2,1,0:T(8,128)(2,1)}), bf16[2,1024,768]{2,1,0:T(8,128)(2,1)}) %all-gather.13.cloned.1.call-update) | async-done | bytes 3145744 | tf_op jit(solution)/shard_map/all_gather | solution.py:175
  160.7 8.7 while.39
  170.8 10.9 %while.40 = (s32[]{:T(128)}, f32[2,128,12,64]{1,3,2,0:T(8,128)}, bf16[2,2,512,12,64]{2,4,3,1,0:T(8,128)(2,1)}, pred[2,2,512]{2,1,0:T(4,128)(4,1)}, bf16[2,2,512,...) while((s32[]{:T(128)}, f32[2,128,12,64]{1,3,2,0:T(8,128)}, ...), condition=%wide.region_5.6_spmd.clone, body=%wide.region_4.5_spmd.clone.sunk | while | flops 409337856 | bytes 5133938 | solution.py:89
  186.9 83.1 %all-gather.17.cloned.1.call-done = bf16[768,3072]{1,0:T(8,128)(2,1)} async-done(((bf16[192,3072]{1,0:T(8,128)(2,1)}), bf16[768,3072]{1,0:T(8,128)(2,1)}) %all-gather.17.cloned.1.call-update) | async-done | bytes 4718608 | tf_op jit(solution)/shard_map/all_gather | solution.py:150
  269.9 6.5 multiply_convert_fusion.1
  276.5 82.8 %all-gather.19.cloned.1.call-done = bf16[3072,768]{1,0:T(8,128)(2,1)} async-done(((bf16[768,768]{1,0:T(8,128)(2,1)}), bf16[3072,768]{1,0:T(8,128)(2,1)}) %all-gather.19.cloned.1.call-update) | async-done | bytes 4718608 | tf_op jit(solution)/shard_map/all_gather | solution.py:152
  372.8 7.2 fusion.158
  390.0 25.8 %while.41 = (s32[]{:T(128)}, f32[2,128,12,64]{1,3,2,0:T(8,128)}, bf16[2,2,512,12,64]{2,4,3,1,0:T(8,128)(2,1)}, bf16[2,2,512,12,64]{2,4,3,1,0:T(8,128)(2,1)}, bf1...) while((s32[]{:T(128)}, f32[2,128,12,64]{1,3,2,0:T(8,128)}, ...), condition=%wide.region_18.19_spmd.clone, body=%wide.region_17.18_spmd.clone.sunk | while | flops 1022754816 | bytes 113400248 | solution.py:125
  415.8 5.1 copy.87
  429.9 5.1 copy.85
  446.5 30.7 %reduce-scatter.15.cloned.1.call-done = bf16[2,128,768]{2,1,0:T(8,128)(2,1)} async-done(((bf16[2,1024,768]{2,1,0:T(8,128)(2,1)}), bf16[2,128,768]{2,1,0:T(8,128)(2,1)}) %reduce-scatter.15.cloned.1.call-update) | async-done | bytes 393232 | tf_op jit(solution)/shard_map/reduce_scatter | solution.py:244
  477.2 50.0 %reduce-scatter.13.cloned.1.call-done = bf16[2,128,768]{2,1,0:T(8,128)(2,1)} async-done(((bf16[2,1024,768]{2,1,0:T(8,128)(2,1)}), bf16[2,128,768]{2,1,0:T(8,128)(2,1)}) %reduce-scatter.13.cloned.1.call-update) | async-done | bytes 393232 | tf_op jit(solution)/shard_map/reduce_scatter | solution.py:241
  550.5 49.5 %reduce-scatter.25.cloned.1.call-done = bf16[192,2304]{1,0:T(8,128)(2,1)} async-done(((bf16[768,2304]{1,0:T(8,128)(2,1)}), bf16[192,2304]{1,0:T(8,128)(2,1)}) %reduce-scatter.25.cloned.1.call-update) | async-done | bytes 884752
  602.3 28.2 %reduce-scatter.17.cloned.1.call-done = bf16[192,768]{1,0:T(8,128)(2,1)} async-done(((bf16[768,768]{1,0:T(8,128)(2,1)}), bf16[192,768]{1,0:T(8,128)(2,1)}) %reduce-scatter.17.cloned.1.call-update) | async-done | bytes 294928 | tf_op jit(solution)/shard_map/reduce_scatter | solution.py:274
  630.5 88.3 %reduce-scatter.19.cloned.1.call-done = bf16[192,3072]{1,0:T(8,128)(2,1)} async-done(((bf16[768,3072]{1,0:T(8,128)(2,1)}), bf16[192,3072]{1,0:T(8,128)(2,1)}) %reduce-scatter.19.cloned.1.call-update) | async-done | bytes 1179664 | tf_op jit(solution)/shard_map/reduce_scatter | solution.py:277
  718.8 88.0 %reduce-scatter.21.cloned.1.call-done = bf16[768,768]{1,0:T(8,128)(2,1)} async-done(((bf16[3072,768]{1,0:T(8,128)(2,1)}), bf16[768,768]{1,0:T(8,128)(2,1)}) %reduce-scatter.21.cloned.1.call-update) | async-done | bytes 1179664 | tf_op jit(solution)/shard_map/reduce_scatter | solution.py:283
  808.8 9.5 %all-reduce = bf16[3072]{0:T(1024)(128)(2,1)S(1)} all-reduce(bf16[3072]{0:T(1024)(128)(2,1)S(1)} %copy-done.54), channel_id=7, replica_groups=mesh['ctx'=8,'wa'=4] {'wa'}, use_global_device_ids=true, to_apply=%region_28.29.clone | all-reduce | flops 3072 | bytes 12288
  827.5 19.5 %reduce-scatter.23.cloned.1.call-done = bf16[192,128]{1,0:T(8,128)(2,1)} async-done(((bf16[768,128]{1,0:T(8,128)(2,1)}), bf16[192,128]{1,0:T(8,128)(2,1)}) %reduce-scatter.23.cloned.1.call-update) | async-done | bytes 49168 | tf_op jit(solution)/shard_map/reduce_scatter | solution.py:286
  847.0 24.3 %all-reduce.1 = (bf16[768]{0:T(1024)(128)(2,1)S(1)}, bf16[192,128]{1,0:T(8,128)(2,1)S(1)}, bf16[8,192]{1,0:T(8,128)(2,1)S(1)}) all-reduce(bf16[768]{0:T(1024)(128)(2,1)S(1)} %dynamic-slice.1, bf16[192,128]{1,0:T(8,128)(2,1)} %reduce-scatter.23.cloned.1.call-done, bf16[8,192]{1,0:T(8,128)(2,1)S(1)} %copy.107), channel_id=1, replica_groups=mesh['ctx'=8,'wa'=4] {'ctx'}, use_global_device_ids=true, to_apply=%region_29.30 | all-reduce | flops 26880 | bytes 107520 | tf_op jit(solution)/shard_map/psum | solution.py:297
  873.2 57.8 %all-reduce.5.cloned.1.call-done = (bf16[192,2304]{0,1:T(8,128)(2,1)}, bf16[192,768]{1,0:T(8,128)(2,1)}, bf16[192,3072]{1,0:T(8,128)(2,1)}, bf16[768,768]{1,0:T(8,128)(2,1)}) async-done(((bf16[192,2304]{0,1:T(8,128)(2,1)}, bf16[192,768]{1,0:T(8,128)(2,1)}, bf16[192,3072]{1,0:T(8,128)(2,1)}, bf16[768,768]{1,0:T(8,128)(2,1)}), (bf16[192,2304]{0,1:T(8,128)(2,1)}, bf16[192,768]{1,0:T(8,128)(2,1)}, ...) | async-done | bytes 3538960 | tf_op jit(solution)/shard_map/psum | solution.py:294
  (314 shorter events, 173.1 us)
Async XLA Ops:
  7.2 71.0 %all-gather.9.cloned.1.call-start = ((), (), s32[]{:S(2)}) async-start(), calls=%async_computation.8 | async-start | bytes 4423680 | tf_op jit(solution)/shard_map/all_gather | solution.py:148
  7.9 108.8 %all-gather.11.cloned.1.call-start = ((), (), s32[]{:S(2)}) async-start(), calls=%async_computation.9 | async-start | bytes 3538944 | tf_op jit(solution)/shard_map/all_gather | solution.py:176
  81.5 19.8 %copy-start.36 = (bf16[192,128]{1,0:T(8,128)(2,1)S(1)}, bf16[192,128]{1,0:T(8,128)(2,1)}, u32[]{:S(2)}) copy-start(bf16[192,128]{1,0:T(8,128)(2,1)} %param.25) | copy-start | bytes 147460
  82.4 68.4 %all-gather.13.cloned.1.call-start = ((), (), s32[]{:S(2)}) async-start(), calls=%async_computation.10 | async-start | bytes 3538944 | tf_op jit(solution)/shard_map/all_gather | solution.py:175
  83.2 100.5 %all-gather.15.cloned.1.call-start = ((), (), s32[]{:S(2)}) async-start(), calls=%async_computation.11 | async-start | bytes 1474560 | tf_op jit(solution)/shard_map/all_gather | solution.py:149
  83.8 186.1 %all-gather.17.cloned.1.call-start = ((), (), s32[]{:S(2)}) async-start(), calls=%async_computation.12 | async-start | bytes 5898240 | tf_op jit(solution)/shard_map/all_gather | solution.py:150
  84.4 274.9 %all-gather.19.cloned.1.call-start = ((), (), s32[]{:S(2)}) async-start(), calls=%async_computation.13 | async-start | bytes 5898240 | tf_op jit(solution)/shard_map/all_gather | solution.py:152
  85.0 392.2 %reduce-scatter.15.cloned.1.call-start = ((), (), s32[]{:S(2)}) async-start(), calls=%async_computation.15 | async-start | bytes 3538944 | tf_op jit(solution)/shard_map/reduce_scatter | solution.py:244
  181.7 88.2 %copy-start.33 = (f32[768]{0:T(1024)S(1)}, f32[768]{0:T(1024)}, u32[]{:S(2)}) copy-start(f32[768]{0:T(1024)} %get-tuple-element.336) | copy-start | bytes 9220
  181.7 88.2 %copy-start.34 = (f32[768]{0:T(1024)S(1)}, f32[768]{0:T(1024)}, u32[]{:S(2)}) copy-start(f32[768]{0:T(1024)} %get-tuple-element.335) | copy-start | bytes 9220
  185.8 194.2 %copy-start.38 = (f32[2,128]{1,0:T(2,128)}, f32[2,128]{1,0:T(2,128)S(1)}, u32[]{:S(2)}) copy-start(f32[2,128]{1,0:T(2,128)S(1)} %broadcast_multiply_fusion.5) | copy-start | bytes 3076
  186.9 89.6 %copy-start.48 = (f32[2,128]{1,0:T(2,128)}, f32[2,128]{1,0:T(2,128)S(1)}, u32[]{:S(2)}) copy-start(f32[2,128]{1,0:T(2,128)S(1)} %add_rsqrt_fusion.2) | copy-start | bytes 3076
  429.6 97.6 %reduce-scatter.13.cloned.1.call-start = ((), (), s32[]{:S(2)}) async-start(), calls=%async_computation.14 | async-start | bytes 3538944 | tf_op jit(solution)/shard_map/reduce_scatter | solution.py:241
  443.7 156.4 %reduce-scatter.25.cloned.1.call-start = ((), (), s32[]{:S(2)}) async-start(), calls=%async_computation.20 | async-start | bytes 4423680
  533.7 96.8 %reduce-scatter.17.cloned.1.call-start = ((), (), s32[]{:S(2)}) async-start(), calls=%async_computation.16 | async-start | bytes 1474560 | tf_op jit(solution)/shard_map/reduce_scatter | solution.py:274
  536.4 182.4 %reduce-scatter.19.cloned.1.call-start = ((), (), s32[]{:S(2)}) async-start(), calls=%async_computation.17 | async-start | bytes 5898240 | tf_op jit(solution)/shard_map/reduce_scatter | solution.py:277
  541.0 265.8 %reduce-scatter.21.cloned.1.call-start = ((), (), s32[]{:S(2)}) async-start(), calls=%async_computation.18 | async-start | bytes 5898240 | tf_op jit(solution)/shard_map/reduce_scatter | solution.py:283
  546.4 280.3 %reduce-scatter.27.cloned.1.call-start = ((), (), s32[]{:S(2)}) async-start(), calls=%async_computation.21 | async-start | bytes 245760
  548.3 298.8 %reduce-scatter.23.cloned.1.call-start = ((), (), s32[]{:S(2)}) async-start(), calls=%async_computation.19 | async-start | bytes 245760 | tf_op jit(solution)/shard_map/reduce_scatter | solution.py:286
  550.4 256.4 %copy-start.64 = (u32[32]{0:T(128)S(1)}, u32[32]{0:T(128)}, u32[]{:S(2)}) copy-start(u32[32]{0:T(128)} %constant.101) | copy-start | bytes 388
  550.5 258.4 %copy-start.54 = (bf16[3072]{0:T(1024)(128)(2,1)S(1)}, bf16[3072]{0:T(1024)(128)(2,1)}, u32[]{:S(2)}) copy-start(bf16[3072]{0:T(1024)(128)(2,1)} %get-tuple-element.415) | copy-start | bytes 18436
  550.5 267.9 %copy-start.30 = (bf16[2,128,768]{2,1,0:T(8,128)(2,1)S(1)}, bf16[2,128,768]{2,1,0:T(8,128)(2,1)}, u32[]{:S(2)}) copy-start(bf16[2,128,768]{2,1,0:T(8,128)(2,1)} %copy.89) | copy-start | bytes 1179652
  550.5 267.9 %copy-start.62 = (bf16[2,128,768]{2,1,0:T(8,128)(2,1)S(1)}, bf16[2,128,768]{2,1,0:T(8,128)(2,1)}, u32[]{:S(2)}) copy-start(bf16[2,128,768]{2,1,0:T(8,128)(2,1)} %reduce-scatter.13.cloned.1.call-done) | copy-start | bytes 1179652
  550.5 380.4 %all-reduce.5.cloned.1.call-start = ((), (), s32[]{:S(2)}) async-start(), calls=%async_computation.22 | async-start | bytes 7667712 | tf_op jit(solution)/shard_map/psum | solution.py:294
  (70 other events, 207.1 us)
Sparse Core Ops, SparseCore 0:
  9.6 68.5 all-gather.8
  82.5 33.4 all-gather.10
  118.5 32.2 all-gather.12
  152.2 29.9 all-gather.14
  183.6 86.2 all-gather.16
  271.4 87.8 all-gather.18
  429.7 47.4 reduce-scatter.14
  480.9 46.2 reduce-scatter.12
  533.8 66.1 reduce-scatter.24
  602.8 27.7 reduce-scatter.16
  632.8 85.9 reduce-scatter.18
  721.0 85.7 reduce-scatter.20
  809.6 17.0 reduce-scatter.26
  829.5 17.5 reduce-scatter.22
  851.2 79.6 all-reduce.4
where the time goes:
time: 954 us; the launch traced here: 945 us
  waiting for transfers between devices  663 us (69%)
  local copies, waits for them, and re-layouts  86.6 us (9%)
  matrix products  78.4 us (8%)
  blocking collectives  74.9 us (8%)
  other arithmetic  24.5 us (3%)
  between operations  15.8 us (2%)
    reduce_scatter x1, waiting for transfers between devices, body(): lax.psum_scatter(up_grad.astype(jnp.bfloat16), 'wa', scatter_dimension=0,...  88.3 us
    reduce_scatter x1, waiting for transfers between devices, body(): lax.psum_scatter(down_grad.astype(jnp.bfloat16), 'wa', scatter_dimension=...  88 us
    all_gather x1, waiting for transfers between devices, body(): lax.all_gather(up_weight, 'wa', axis=0, tiled=True)  83.1 us
    all_gather x1, waiting for transfers between devices, body(): lax.all_gather(down_weight, 'wa', axis=0, tiled=True)  82.8 us
    psum x1, waiting for transfers between devices, body(): lax.psum(owned[0].astype(jnp.bfloat16), 'ctx').astype(jnp.float32)  57.8 us
    unnamed x17, waiting for transfers between devices  56.2 us
    all_gather x1, waiting for transfers between devices, body(): lax.all_gather(qkv_weight, 'wa', axis=0, tiled=True)  56 us
    reduce_scatter x1, waiting for transfers between devices, body(): lax.psum_scatter(key_terms.astype(jnp.bfloat16), 'ctx', scatter_dimension...  50 us
  transfers between devices with their start and end apart: 15, of which 13 were waited for; matrix products, arithmetic and copies ran while one was open for 10% of the time, Pallas kernels for 0%

commit v1 on v0

--- a/solution.py
+++ b/solution.py
@@ -131,7 +131,7 @@
     )
 
 
-def body(
+def general_body(
     tokens,
     doc_lengths,
     group_deal,
@@ -312,6 +312,404 @@
     )
 
 
+PLANE = 8
+LINE = 4
+ORDER = (0, 4, 2, 6, 1, 5, 3, 7)
+F32 = jnp.float32
+BF16 = jnp.bfloat16
+
+
+def plane_swap(array, bits):
+    return lax.ppermute(array, "ctx", [(i, i ^ bits) for i in range(PLANE)])
+
+
+def line_turn(array, step):
+    return lax.ppermute(array, "wa", [(i, (i + step) % LINE) for i in range(LINE)])
+
+
+def line_turns(array):
+    return [line_turn(array, step) for step in range(1, LINE)]
+
+
+def relay(from_x, from_y, core):
+    passed = jnp.where(core == 0, from_y, from_x)
+    pairs = [(i, i ^ 2 if i % 2 == 0 else i ^ 4) for i in range(PLANE)]
+    return lax.ppermute(passed, "ctx", pairs)
+
+
+def pick(array, index):
+    return lax.dynamic_index_in_dim(array, index, 0, keepdims=False)
+
+
+def dot(left, right, dims):
+    return lax.dot_general(left, right, (dims, ((), ())), preferred_element_type=F32)
+
+
+NN = ((1,), (0,))
+NT = ((1,), (1,))
+TN = ((0,), (0,))
+
+
+def norm_forward(rows):
+    middle = jnp.mean(rows, axis=-1, keepdims=True)
+    center = rows - middle
+    scaled = lax.rsqrt(jnp.mean(center * center, axis=-1, keepdims=True) + NORM_EPS)
+    return center * scaled, scaled
+
+
+def norm_reverse(grad, unit, scaled, gain):
+    inner = grad * gain
+    return scaled * (
+        inner
+        - jnp.mean(inner, axis=-1, keepdims=True)
+        - unit * jnp.mean(inner * unit, axis=-1, keepdims=True)
+    )
+
+
+def plane_body(
+    tokens,
+    doc_lengths,
+    group_deal,
+    qkv_weight,
+    out_weight,
+    up_weight,
+    up_bias,
+    down_weight,
+    proj_weight,
+    vectors,
+    cotangent,
+):
+    me = lax.axis_index("ctx")
+    line = lax.axis_index("wa")
+    y, core, group = me // 4, me % 2, me % 4
+    seq_count, span, width = tokens.shape
+    shard = width // LINE
+    inner_shard = up_weight.shape[1] // LINE
+    piece = inner_shard // PLANE
+    half = shard // 2
+    wide = H * HEAD // 4
+
+    mine, other = pick(tokens, y), pick(tokens, 1 - y)
+    got_y = plane_swap(other, 4)
+    got_x = plane_swap(mine, 2)
+    got_d = plane_swap(other, 6)
+    near = jnp.stack([mine, got_y, got_x, got_d])
+    far = plane_swap(near, 1)
+    slots = jnp.concatenate([near, far]).reshape(PLANE * span, width)
+
+    own_cols = jnp.concatenate(
+        [
+            lax.dynamic_slice(qkv_weight, (0, part * width + group * wide), (shard, wide))
+            for part in range(3)
+        ]
+        + [vectors.T, up_bias.reshape(LINE, shard).T, jnp.zeros((shard, 64 - 12), BF16)],
+        axis=1,
+    )
+    half_rows = lax.dynamic_slice(own_cols, (y * half, 0), (half, own_cols.shape[1]))
+    line_halves = jnp.stack(line_turns(half_rows))
+    other_halves = plane_swap(line_halves, 4)
+    low_half = jnp.where(y == 0, line_halves, other_halves)
+    high_half = jnp.where(y == 0, other_halves, line_halves)
+    cols_by_turn = jnp.concatenate(
+        [own_cols[None], jnp.concatenate([low_half, high_half], axis=1)]
+    )
+
+    def by_line(turned):
+        return jnp.concatenate([pick(turned, (line - a) % LINE)[None] for a in range(LINE)])
+
+    cols = by_line(cols_by_turn).reshape(width, -1)
+    qkv_cols = cols[:, : 3 * wide]
+    small = cols[:, 3 * wide :]
+    vector_full = small[:, :8].T.astype(F32)
+    bias_full = small[:, 8:12].reshape(LINE, shard, 4).transpose(0, 2, 1).reshape(-1)
+    bias_parts = bias_full.reshape(LINE, PLANE, piece).transpose(1, 0, 2).reshape(PLANE, -1)
+
+    up_own = jnp.concatenate(
+        [
+            lax.dynamic_slice(up_weight, (0, s * inner_shard + me * piece), (shard, piece))
+            for s in range(LINE)
+        ],
+        axis=1,
+    )
+    eighth = shard // PLANE
+    out_own = lax.dynamic_slice(out_weight, (me * eighth, 0), (eighth, width))
+    first_own = jnp.concatenate([up_own, out_own[:, : width // 2], out_own[:, width // 2 :]])
+    down_own = lax.dynamic_slice(down_weight, (me * piece, 0), (piece, width))
+    proj_own = lax.dynamic_slice(proj_weight, (me * eighth, 0), (eighth, 128))
+    second_own = jnp.concatenate(
+        [down_own, proj_own.reshape(-1, width), jnp.zeros((12, width), BF16)]
+    )
+
+    def over_plane(turns):
+        stacked = jnp.stack(turns)
+        from_x = plane_swap(stacked, 2)
+        from_y = plane_swap(stacked, 4)
+        from_d = relay(from_x, from_y, core)
+        close = [stacked, from_y, from_x, from_d]
+        return close + [plane_swap(part, 1) for part in close]
+
+    first_turns = line_turns(first_own)
+    second_turns = line_turns(second_own)
+    first_parts = over_plane(first_turns)
+    second_parts = over_plane(second_turns)
+
+    up_all = (
+        up_weight.reshape(shard, LINE, PLANE, piece).transpose(2, 0, 1, 3).reshape(PLANE, shard, -1)
+    )
+    down_all = down_weight.reshape(PLANE, piece, width)
+    ups, downs = [], []
+    for place, bits in enumerate(ORDER):
+        ups.append(
+            by_line(
+                jnp.concatenate([pick(up_all, me ^ bits)[None], first_parts[place][:, :shard]])
+            ).reshape(width, -1)
+        )
+        downs.append(
+            by_line(
+                jnp.concatenate([pick(down_all, me ^ bits)[None], second_parts[place][:, :piece]])
+            ).reshape(-1, width)
+        )
+    out_rel = jnp.stack(
+        [
+            jnp.concatenate([p[:, shard : shard + eighth], p[:, shard + eighth :]], axis=2)
+            for p in first_parts
+        ]
+    )
+    proj_rel = jnp.stack([p[:, piece : piece + 4].reshape(3, eighth, 128) for p in second_parts])
+
+    def whole(own, rel):
+        ordered = jnp.stack([pick(rel, jnp.asarray(inverse_order)[me ^ b]) for b in range(PLANE)], 1)
+        turned = jnp.concatenate([own[None], ordered.reshape(3, own.shape[0], -1)])
+        return by_line(turned).reshape(LINE * own.shape[0], -1)
+
+    inverse_order = [ORDER.index(b) for b in range(PLANE)]
+    out_full = whole(out_weight, out_rel)
+    proj_full = whole(proj_weight, proj_rel)
+
+    seq = line * seq_count + y
+    length = pick(doc_lengths, seq)
+    deal_row = pick(group_deal, seq)
+    blocks = jnp.stack([pick(deal_row, me ^ bits) for bits in ORDER])
+    valid = (blocks[:, None] * span + jnp.arange(span, dtype=jnp.int32)[None, :]) < length
+    valid = valid.reshape(1, PLANE * span)
+
+    mixed = dot(slots, qkv_cols, NN)
+    scale = HEAD ** (-0.5)
+    q_bias = lax.dynamic_slice(vector_full, (0, group * wide), (1, wide))
+    v_bias = lax.dynamic_slice(vector_full, (1, group * wide), (1, wide))
+    queries = ((mixed[:, :wide] + q_bias) * scale).astype(BF16)
+    keys = mixed[:, wide : 2 * wide].astype(BF16)
+    values = (mixed[:, 2 * wide :] + v_bias).astype(BF16)
+    heads = wide // HEAD
+    attended, probs_kept = [], []
+    for h in range(heads):
+        cut = slice(h * HEAD, (h + 1) * HEAD)
+        scores = jnp.where(valid, dot(queries[:, cut], keys[:, cut], NT), NEG_FILL)
+        raised = jnp.exp(scores - jnp.max(scores, axis=-1, keepdims=True))
+        probs = raised / jnp.sum(raised, axis=-1, keepdims=True)
+        probs_kept.append(probs)
+        attended.append(dot(probs.astype(BF16), values[:, cut], NN))
+    attended_f = jnp.concatenate(attended, axis=1)
+    sent = attended_f.astype(BF16).reshape(4, 2 * span, wide)
+    near_bits = (0, 2, 1, 3)
+    attended_low = [sent[0]] + [plane_swap(sent[i], near_bits[i]) for i in (1, 2, 3)]
+
+    own_slots = slots[: 2 * span].astype(F32)
+    first_sum = own_slots + vector_full[2]
+    out_groups = out_full.reshape(4, wide, width)
+    for i, bits in enumerate(near_bits):
+        first_sum = first_sum + dot(attended_low[i], pick(out_groups, group ^ bits), NN)
+    unit_one, scale_one = norm_forward(first_sum)
+    normed = unit_one * vector_full[3] + vector_full[4]
+    normed_low = normed.astype(BF16)
+
+    def gather_plane(array):
+        from_y = plane_swap(array, 4)
+        from_x = plane_swap(array, 2)
+        from_d = plane_swap(array, 6)
+        close = jnp.concatenate([array, from_y, from_x, from_d])
+        return jnp.concatenate([close, plane_swap(close, 1)])
+
+    normed_plane = gather_plane(normed_low)
+
+    inner_sums, actives = [], []
+    second_sum = normed + vector_full[5]
+    for place, bits in enumerate(ORDER):
+        inner = dot(normed_low, ups[place], NN) + pick(bias_parts, me ^ bits).astype(F32)
+        active, slope = gelu_both(inner)
+        inner_sums.append(slope)
+        second_sum = second_sum + dot(active.astype(BF16), downs[place], NN)
+    unit_two, scale_two = norm_forward(second_sum)
+    final_low = (unit_two * vector_full[6] + vector_full[7]).astype(BF16)
+    project = dot(final_low, proj_full, NN)
+    inverse = lax.rsqrt(jnp.sum(project * project, axis=-1, keepdims=True) + NORM_EPS)
+    direction = project * inverse
+    cot_mine, cot_other = pick(cotangent, y), pick(cotangent, 1 - y)
+    own_cot = jnp.concatenate([cot_mine, plane_swap(cot_other, 4)]).astype(F32)
+    row_mask = valid[0, : 2 * span].astype(F32)[:, None]
+    embedded = (direction * row_mask).astype(BF16)
+    upstream = own_cot * row_mask
+    project_grad = (
+        inverse * (upstream - direction * jnp.sum(upstream * direction, axis=-1, keepdims=True))
+    ).astype(BF16)
+    embed_other = plane_swap(embedded[span:], 4)
+    embeddings = jnp.where(
+        y == 0,
+        jnp.stack([embedded[:span], embed_other]),
+        jnp.stack([embed_other, embedded[:span]]),
+    )
+    proj_part = dot(final_low, project_grad, TN)
+    final_grad = dot(project_grad, proj_full, NT)
+    second_grad = norm_reverse(final_grad, unit_two, scale_two, vector_full[6])
+    down_low = second_grad.astype(BF16)
+    down_plane = gather_plane(down_low)
+
+    normed_grad = second_grad
+    bias_part = jnp.zeros((PLANE, 4 * piece), F32)
+    for place, bits in enumerate(ORDER):
+        inner_grad = dot(down_low, downs[place], NT) * inner_sums[place]
+        bias_part = lax.dynamic_update_slice(
+            bias_part, jnp.sum(inner_grad, axis=0, keepdims=True), (me ^ bits, 0)
+        )
+        normed_grad = normed_grad + dot(inner_grad.astype(BF16), ups[place], NT)
+    first_grad = norm_reverse(normed_grad, unit_one, scale_one, vector_full[3])
+    first_low = first_grad.astype(BF16)
+    attended_all = jnp.zeros((4, 2 * span, wide), BF16)
+    for i, bits in enumerate(near_bits):
+        attended_all = lax.dynamic_update_slice(
+            attended_all, attended_low[i][None], (group ^ bits, 0, 0)
+        )
+    out_part = jnp.concatenate([dot(attended_all[g], first_low, TN) for g in range(4)])
+    grad_sent = [
+        dot(first_low, pick(out_groups, group ^ bits), NT).astype(BF16) for bits in near_bits
+    ]
+    attended_grad = jnp.concatenate(
+        [grad_sent[0]] + [plane_swap(grad_sent[i], near_bits[i]) for i in (1, 2, 3)]
+    )
+
+    bias_rows = bias_part.reshape(PLANE, LINE, piece).transpose(1, 0, 2).reshape(LINE, 4, shard)
+    bias_rows = bias_rows.transpose(0, 2, 1).reshape(width, 4)
+    sums = jnp.stack(
+        [
+            jnp.sum(first_grad, axis=0),
+            jnp.sum(normed_grad * unit_one, axis=0),
+            jnp.sum(normed_grad, axis=0),
+            jnp.sum(second_grad, axis=0),
+            jnp.sum(final_grad * unit_two, axis=0),
+            jnp.sum(final_grad, axis=0),
+        ],
+        axis=1,
+    )
+    rest = jnp.concatenate(
+        [out_part, proj_part, sums, bias_rows, jnp.zeros((width, 128 - 10), F32)], axis=1
+    ).astype(BF16)
+    rest = lax.psum_scatter(rest, "wa", scatter_dimension=0, tiled=True)
+    rest = lax.psum(rest, "ctx").astype(F32)
+    out_grad = rest[:, :width]
+    proj_grad = rest[:, width : width + 128]
+    bias_grad = rest[:, width + 134 : width + 138].T.reshape(-1)
+    late_rows = rest[:, width + 128 : width + 134].T
+
+    inner = dot(normed_plane, ups[0], NN) + pick(bias_parts, me).astype(F32)
+    active, slope = gelu_both(inner)
+    inner_low = (dot(down_plane, downs[0], NT) * slope).astype(BF16)
+    up_part = dot(normed_plane, inner_low, TN).astype(BF16).reshape(LINE, shard, -1)
+    down_part = dot(active.astype(BF16), down_plane, TN).astype(BF16)
+    down_part = down_part.reshape(LINE, piece, width)
+
+    def sum_line(parts):
+        total = pick(parts, line).astype(F32)
+        for step in range(1, LINE):
+            total = total + line_turn(pick(parts, (line + step) % LINE), step).astype(F32)
+        return total.astype(BF16)
+
+    def share_plane(array):
+        from_x = plane_swap(array, 2)
+        from_y = plane_swap(array, 4)
+        from_d = plane_swap(array, 6)
+        close = jnp.stack([array, from_y, from_x, from_d])
+        both = jnp.concatenate([close, plane_swap(close, 1)])
+        return jnp.stack([pick(both, jnp.asarray(inverse_order)[me ^ b]) for b in range(PLANE)])
+
+    up_mine = share_plane(sum_line(up_part))
+    down_mine = share_plane(sum_line(down_part))
+    up_grad = (
+        up_mine.reshape(PLANE, shard, LINE, piece)
+        .transpose(1, 2, 0, 3)
+        .reshape(shard, -1)
+        .astype(F32)
+    )
+    down_grad = down_mine.reshape(-1, width).astype(F32)
+
+    query_parts, key_parts, value_parts = [], [], []
+    for h in range(heads):
+        cut = slice(h * HEAD, (h + 1) * HEAD)
+        probs = probs_kept[h]
+        grad_h = attended_grad[:, cut]
+        prob_grad = dot(grad_h, values[:, cut], NT)
+        delta = jnp.sum(grad_h.astype(F32) * attended[h], axis=-1, keepdims=True)
+        score_low = (probs * (prob_grad - delta)).astype(BF16)
+        query_parts.append(dot(score_low, keys[:, cut], NN).astype(BF16) * BF16(scale))
+        key_parts.append(dot(score_low, queries[:, cut], TN).astype(BF16))
+        value_parts.append(dot(probs.astype(BF16), grad_h, TN).astype(BF16))
+    mixed_grad = jnp.concatenate(query_parts + key_parts + value_parts, axis=1)
+    qkv_part = dot(slots, mixed_grad, TN).astype(BF16).reshape(LINE, 2, half, 3 * wide)
+    column_sums = jnp.sum(mixed_grad.astype(F32), axis=0).astype(BF16)
+    extra = jnp.concatenate(
+        [column_sums[None], jnp.zeros((15, 3 * wide), BF16)]
+    )
+    extra = jnp.broadcast_to(extra[None], (LINE, 16, 3 * wide))
+    half_mine = jnp.concatenate([jnp.where(y == 0, qkv_part[:, 0], qkv_part[:, 1]), extra], axis=1)
+    half_other = jnp.concatenate([jnp.where(y == 0, qkv_part[:, 1], qkv_part[:, 0]), extra], axis=1)
+    half_sum = (half_mine.astype(F32) + plane_swap(half_other, 4).astype(F32)).astype(BF16)
+    qkv_mine = share_plane(sum_line(half_sum))
+    qkv_grad = (
+        qkv_mine[:, :half]
+        .reshape(2, 4, half, 3, wide)
+        .transpose(0, 2, 3, 1, 4)
+        .reshape(shard, 3 * width)
+        .astype(F32)
+    )
+    group_sums = pick(qkv_mine[:4, half], line).astype(F32)
+    early_rows = jnp.stack([group_sums[:wide], group_sums[2 * wide :]])
+    vectors_grad = jnp.concatenate([early_rows, late_rows])
+
+    token_part = dot(mixed_grad, qkv_cols, NT).reshape(PLANE, span, width)
+    near_sum = token_part[:4] + plane_swap(token_part[4:].astype(BF16), 1).astype(F32)
+    kept = near_sum[0] + first_grad[:span]
+    passed = near_sum[1] + first_grad[span:]
+    for_mine = kept + plane_swap(near_sum[2].astype(BF16), 2).astype(F32)
+    for_other = plane_swap(passed.astype(BF16), 4).astype(F32) + plane_swap(
+        near_sum[3].astype(BF16), 6
+    ).astype(F32)
+    tokens_grad = jnp.where(
+        y == 0, jnp.stack([for_mine, for_other]), jnp.stack([for_other, for_mine])
+    )
+    return (
+        embeddings,
+        tokens_grad,
+        qkv_grad,
+        out_grad,
+        up_grad,
+        bias_grad,
+        down_grad,
+        proj_grad,
+        vectors_grad,
+    )
+
+
+def body(*arrays):
+    sequences, span, width = arrays[0].shape
+    fits = (
+        lax.axis_size("ctx") == PLANE
+        and lax.axis_size("wa") == LINE
+        and sequences == 2
+        and span == 128
+        and width == H * HEAD
+    )
+    return (plane_body if fits else general_body)(*arrays)
+
+
 def solution(mesh):
     in_specs = (
         P("wa", "ctx", None),

time: 954 us -> 525 us (0.55)
  waiting for transfers between devices: 663 us -> 120 us
  blocking collectives: 74.9 us -> 0 us
  starting transfers between devices: 0.86 us -> 72.5 us
  local copies, waits for them, and re-layouts: 86.6 us -> 145 us
  other arithmetic: 24.5 us -> 68.3 us
  between operations: 15.8 us -> 32.5 us
    reduce_scatter x6 -> x1, waiting for transfers between devices: 305 us -> 0.02 us  [plane_body(): rest = lax.psum_scatter(rest, 'wa', scatter_dimension=0, tiled=True)]
    all_gather x6 -> x0, waiting for transfers between devices: 244 us -> none  [the longest x1 83.1 us: body(): lax.all_gather(up_weight, 'wa', axis=0, tiled=True)]
    ppermute x0 -> x70, starting transfers between devices: none -> 72.2 us  [the longest x50 41.5 us: plane_swap(): return lax.ppermute(array, 'ctx', [(i, i ^ bits) for i in range(PLANE)])]
    ppermute x0 -> x70, waiting for transfers between devices: none -> 68.6 us  [the longest x50 47.6 us: plane_swap(): return lax.ppermute(array, 'ctx', [(i, i ^ bits) for i in range(PLANE)])]
    unnamed x17 -> x2, waiting for transfers between devices: 56.2 us -> 0.03 us
    all_gather x3 -> x0, blocking collectives: 41.1 us -> none  [the longest x1 14.5 us: body(): lax.all_gather(proj_weight, 'wa', axis=0, tiled=True)]
    slice x1 -> x43, local copies, waits for them, and re-layouts: 0.79 us -> 30.6 us  [the longest x9 7.39 us: plane_body(): second_parts[place][:, :piece]]
    concatenate x0 -> x48, other arithmetic: none -> 26.2 us  [the longest x19 11.7 us: by_line(): jnp.concatenate([pick(turned, (line - a) % LINE)[None] for a in range(LIN...]
  transfers between devices with their start and end apart: 15 -> 72, of which waited for: 13 -> 18; matrix products, arithmetic and copies ran while one was open for 10% -> 47% of each run, Pallas kernels for 0% -> 0%
where the time goes in v1:
time: 525 us; the launch traced here: 514 us
  local copies, waits for them, and re-layouts  145 us (28%)
  waiting for transfers between devices  120 us (23%)
  matrix products  75.4 us (14%)
  starting transfers between devices  72.5 us (14%)
  other arithmetic  68.3 us (13%)
  between operations  32.5 us (6%)
    dot_general x71, matrix products, dot(): lax.dot_general(left, right, (dims, ((), ())), preferred_element_type=F32)  75.4 us
    psum x1, waiting for transfers between devices, plane_body(): rest = lax.psum(rest, 'ctx').astype(F32)  51.8 us
    ppermute x50, waiting for transfers between devices, plane_swap(): return lax.ppermute(array, 'ctx', [(i, i ^ bits) for i in range(PLANE)])  47.6 us
    unnamed x286, local copies, waits for them, and re-layouts  45.3 us
    ppermute x50, starting transfers between devices, plane_swap(): return lax.ppermute(array, 'ctx', [(i, i ^ bits) for i in range(PLANE)])  41.5 us
    ppermute x18, starting transfers between devices, line_turn(): lax.ppermute(array, 'wa', [(i, (i + step) % LINE) for i in range(LINE)])  28.7 us
    ppermute x18, waiting for transfers between devices, line_turn(): lax.ppermute(array, 'wa', [(i, (i + step) % LINE) for i in range(LINE)])  20.9 us
    concatenate x19, other arithmetic, by_line(): jnp.concatenate([pick(turned, (line - a) % LINE)[None] for a in range(LIN...  11.7 us
  transfers between devices with their start and end apart: 72, of which 18 were waited for; matrix products, arithmetic and copies ran while one was open for 47% of the time, Pallas kernels for 0%

profile of v1, /device:TPU:8, one launch (start us, length us, event | category | flops | bytes accessed | tf_op | source)
XLA Modules:
  0.0 514.4 jit_solution(12145009924747686387)
XLA Ops:
  9.8 3.0 collective-permute-start.22
  23.0 5.3 %stack.311 = s32[8]{0:T(128)S(1)} concatenate(s32[1]{0:T(128)} %bitcast.11, s32[1]{0:T(128)} %bitcast.12, s32[1]{0:T(128)} %bitcast.13, s32[1]{0:T(128)} %bitcast.14, s32[1]{0:T(128)} %bitcast.15, s32[1]{0:T(128)} %bitcast.16, s32[1]{0:T(128)} %bitcast.17, s32[1]{0:T(128)} %bitcast.18), dimensions={0} | concatenate | bytes 64 | tf_op jit(solution)/shard_map/stack | solution.py:492
  72.0 3.9 collective-permute-done.10
  93.6 7.3 %collective-permute-done.24 = bf16[3,112,768]{2,1,0:T(8,128)(2,1)} collective-permute-done((bf16[3,112,768]{2,1,0:T(8,128)(2,1)}, bf16[3,112,768]{2,1,0:T(8,128)(2,1)}, u32[]{:S(2)}, u32[]{:S(2)}) %collective-permute-start.24) | collective-permute-done | bytes 516128 | tf_op jit(solution)/shard_map/ppermute | solution.py:323
  146.0 3.2 collective-permute-done.18
  151.6 3.6 collective-permute-done.20
  257.8 4.6 concatenate.286
  272.2 3.1 multiply_convert_fusion.2
  288.0 3.2 fusion.37
  312.7 10.7 %collective-permute-done.40 = bf16[4,112,576]{2,1,0:T(8,128)(2,1)S(1)} collective-permute-done((bf16[4,112,576]{2,1,0:T(8,128)(2,1)S(1)}, bf16[4,112,576]{2,1,0:T(8,128)(2,1)S(1)}, u32[]{:S(2)}, u32[]{:S(2)}) %collective-permute-start.40) | collective-permute-done | bytes 516128 | tf_op jit(solution)/shard_map/ppermute | solution.py:323
  331.1 4.4 collective-permute-done.42
  351.6 5.3 %collective-permute-done.37 = bf16[128,768]{1,0:T(8,128)(2,1)S(1)} collective-permute-done((bf16[128,768]{1,0:T(8,128)(2,1)S(1)}, bf16[128,768]{1,0:T(8,128)(2,1)S(1)}, u32[]{:S(2)}, u32[]{:S(2)}) %collective-permute-start.37) | collective-permute-done | bytes 196640 | tf_op jit(solution)/shard_map/ppermute | solution.py:323
  358.0 3.2 collective-permute-done.39
  361.1 4.1 collective-permute-done.38
  368.7 3.5 convolution_add_fusion
  373.5 7.3 %convolution_convert_fusion.1 = bf16[768,384]{1,0:T(8,128)(2,1)S(1)} fusion(bf16[2048,768]{1,0:T(8,128)(2,1)} %copy-done.92, f32[2048,384]{1,0:T(8,128)} %convolution_add_fusion, bf16[2048,768]{1,0:T(8,128)(2,1)} %constant_dynamic-update-slice_fusion.55, bf16[384,768]{1,0:T(8,128)(2,1)S(1)} %bitcast.441), kind=kOutput, calls=%fused_computation.38 | convolution fusion | flops 2424078336 | bytes 10616832 | tf_op jit(solution)/shard_map/dot_general | solution.py:345
  384.8 4.3 fusion.13
  394.7 6.5 %collective-permute-done.56 = bf16[192,384]{1,0:T(8,128)(2,1)S(1)} collective-permute-done((bf16[192,384]{1,0:T(8,128)(2,1)S(1)}, bf16[192,384]{1,0:T(8,128)(2,1)S(1)}, u32[]{:S(2)}, u32[]{:S(2)}) %collective-permute-start.56) | collective-permute-done | bytes 147488 | tf_op jit(solution)/shard_map/ppermute | solution.py:327
  404.0 3.0 collective-permute-done.65
  417.3 3.7 reshape.405
  436.9 3.3 reshape.411
  440.2 3.5 copy.199
  443.7 4.6 reshape.407
  451.4 51.8 %all-reduce.3.cloned.1.call-done = bf16[192,1024]{1,0:T(8,128)(2,1)} async-done(((bf16[192,1024]{1,0:T(8,128)(2,1)}), bf16[192,1024]{1,0:T(8,128)(2,1)}) %all-reduce.3.cloned.1.call-update) | async-done | bytes 393232 | tf_op jit(solution)/shard_map/psum | solution.py:607
  (736 shorter events, 325.6 us)
Async XLA Ops:
  7.2 442.5 %reduce-scatter.2.cloned.1.call-start = ((), (), s32[]{:S(2)}) async-start(), calls=%async_computation.1 | async-start | bytes 1966080 | tf_op jit(solution)/shard_map/reduce_scatter | solution.py:606
  9.8 51.5 %collective-permute-start.23 = (bf16[112,768]{1,0:T(8,128)(2,1)}, bf16[112,768]{1,0:T(8,128)(2,1)}, u32[]{:S(2)}, u32[]{:S(2)}) collective-permute-start(bf16[112,768]{1,0:T(8,128)(2,1)} %maximum_maximum_fusion.1), channel_id=1, source_target_pairs={{0,3},{1,0},{2,1},{3,2},{4,7},{5,4},{6,5},{7,6},{8,11},{9,8},{10,9... | collective-permute-start | bytes 516104 | tf_op jit(solution)/shard_map/ppermute | solution.py:327
  9.8 51.5 %collective-permute-start.22 = (bf16[112,768]{1,0:T(8,128)(2,1)}, bf16[112,768]{1,0:T(8,128)(2,1)}, u32[]{:S(2)}, u32[]{:S(2)}) collective-permute-start(bf16[112,768]{1,0:T(8,128)(2,1)} %maximum_maximum_fusion.1), channel_id=1, source_target_pairs={{0,2},{1,3},{2,0},{3,1},{4,6},{5,7},{6,4},{7,5},{8,10},{9,11},{10,... | collective-permute-start | bytes 516104 | tf_op jit(solution)/shard_map/ppermute | solution.py:327
  12.9 50.5 %collective-permute-start.21 = (bf16[112,768]{1,0:T(8,128)(2,1)}, bf16[112,768]{1,0:T(8,128)(2,1)}, u32[]{:S(2)}, u32[]{:S(2)}) collective-permute-start(bf16[112,768]{1,0:T(8,128)(2,1)} %maximum_maximum_fusion.1), channel_id=1, source_target_pairs={{0,1},{1,2},{2,3},{3,0},{4,5},{5,6},{6,7},{7,4},{8,9},{9,10},{10,1... | collective-permute-start | bytes 516104 | tf_op jit(solution)/shard_map/ppermute | solution.py:327
  19.2 38.2 %collective-permute-start.2 = (bf16[96,640]{1,0:T(8,128)(2,1)}, bf16[96,640]{1,0:T(8,128)(2,1)S(1)}, u32[]{:S(2)}, u32[]{:S(2)}) collective-permute-start(bf16[96,640]{1,0:T(8,128)(2,1)} %constant_dynamic-slice_fusion.54), channel_id=1, source_target_pairs={{0,2},{1,3},{2,0},{3,1},{4,6},{5,7},{6,4},{7,5},{8,10},{9,11},{10,... | collective-permute-start | bytes 368648 | tf_op jit(solution)/shard_map/ppermute | solution.py:327
  57.5 23.5 %collective-permute-start = (bf16[128,768]{1,0:T(8,128)(2,1)}, bf16[128,768]{1,0:T(8,128)(2,1)S(1)}, u32[]{:S(2)}, u32[]{:S(2)}) collective-permute-start(bf16[128,768]{1,0:T(8,128)(2,1)} %get-tuple-element.242), channel_id=1, source_target_pairs={{0,16},{4,20},{8,24},{12,28},{16,0},{20,4},{24,8},{28,12},{1,17},{... | collective-permute-start | bytes 589832 | tf_op jit(solution)/shard_map/ppermute | solution.py:323
  59.1 25.7 %collective-permute-start.6 = (bf16[128,768]{1,0:T(8,128)(2,1)}, bf16[128,768]{1,0:T(8,128)(2,1)S(1)}, u32[]{:S(2)}, u32[]{:S(2)}) collective-permute-start(bf16[128,768]{1,0:T(8,128)(2,1)} %get-tuple-element.242), channel_id=1, source_target_pairs={{0,24},{4,28},{8,16},{12,20},{16,8},{20,12},{24,0},{28,4},{1,25},{... | collective-permute-start | bytes 589832 | tf_op jit(solution)/shard_map/ppermute | solution.py:323
  76.4 136.4 %collective-permute-start.32 = (bf16[128,128]{0,1:T(8,128)(2,1)}, bf16[128,128]{0,1:T(8,128)(2,1)}, u32[]{:S(2)}, u32[]{:S(2)}) collective-permute-start(bf16[128,128]{0,1:T(8,128)(2,1)} %bitcast.98), channel_id=1, source_target_pairs={{0,16},{4,20},{8,24},{12,28},{16,0},{20,4},{24,8},{28,12},{1,17},{... | collective-permute-start | bytes 98312 | tf_op jit(solution)/shard_map/ppermute | solution.py:323
  89.7 26.9 %collective-permute-start.11 = (bf16[3,240,384]{2,1,0:T(8,128)(2,1)S(1)}, bf16[3,240,384]{2,1,0:T(8,128)(2,1)}, u32[]{:S(2)}, u32[]{:S(2)}) collective-permute-start(bf16[3,240,384]{2,1,0:T(8,128)(2,1)S(1)} %pad_maximum_fusion.27), channel_id=1, source_target_pairs={{0,16},{4,20},{8,24},{12,28},{16,0},{20,4},{24,8},{28,12},{1,17},{... | collective-permute-start | bytes 1658888 | tf_op jit(solution)/shard_map/ppermute | solution.py:323
  105.8 22.3 %collective-permute-start.7 = (bf16[4,128,768]{2,1,0:T(8,128)(2,1)}, bf16[4,128,768]{2,1,0:T(8,128)(2,1)}, u32[]{:S(2)}, u32[]{:S(2)}) collective-permute-start(bf16[4,128,768]{2,1,0:T(8,128)(2,1)} %pad_maximum_fusion.7), channel_id=1, source_target_pairs={{0,4},{4,0},{8,12},{12,8},{16,20},{20,16},{24,28},{28,24},{1,5},{5... | collective-permute-start | bytes 2359304 | tf_op jit(solution)/shard_map/ppermute | solution.py:323
  116.6 40.0 %collective-permute-start.26 = (bf16[3,112,768]{2,1,0:T(8,128)(2,1)S(1)}, bf16[3,112,768]{2,1,0:T(8,128)(2,1)S(1)}, u32[]{:S(2)}, u32[]{:S(2)}) collective-permute-start(bf16[3,112,768]{2,1,0:T(8,128)(2,1)S(1)} %broadcast_select_fusion.1), channel_id=1, source_target_pairs={{0,8},{4,20},{8,0},{12,28},{16,24},{20,4},{24,16},{28,12},{1,9},{5... | collective-permute-start | bytes 1548296 | tf_op jit(solution)/shard_map/ppermute | solution.py:337
  118.4 41.1 %collective-permute-start.28 = (bf16[3,112,768]{2,1,0:T(8,128)(2,1)}, bf16[3,112,768]{2,1,0:T(8,128)(2,1)}, u32[]{:S(2)}, u32[]{:S(2)}) collective-permute-start(bf16[3,112,768]{2,1,0:T(8,128)(2,1)} %collective-permute-done.24), channel_id=1, source_target_pairs={{0,4},{4,0},{8,12},{12,8},{16,20},{20,16},{24,28},{28,24},{1,5},{5... | collective-permute-start | bytes 1548296 | tf_op jit(solution)/shard_map/ppermute | solution.py:323
  119.1 43.1 %collective-permute-start.29 = (bf16[3,112,768]{2,1,0:T(8,128)(2,1)}, bf16[3,112,768]{2,1,0:T(8,128)(2,1)}, u32[]{:S(2)}, u32[]{:S(2)}) collective-permute-start(bf16[3,112,768]{2,1,0:T(8,128)(2,1)} %collective-permute-done.25), channel_id=1, source_target_pairs={{0,4},{4,0},{8,12},{12,8},{16,20},{20,16},{24,28},{28,24},{1,5},{5... | collective-permute-start | bytes 1548296 | tf_op jit(solution)/shard_map/ppermute | solution.py:323
  159.4 22.5 %collective-permute-start.16 = (bf16[3,240,384]{2,1,0:T(8,128)(2,1)}, bf16[3,240,384]{2,1,0:T(8,128)(2,1)}, u32[]{:S(2)}, u32[]{:S(2)}) collective-permute-start(bf16[3,240,384]{2,1,0:T(8,128)(2,1)} %copy-done.27), channel_id=1, source_target_pairs={{0,4},{4,0},{8,12},{12,8},{16,20},{20,16},{24,28},{28,24},{1,5},{5... | collective-permute-start | bytes 1658888 | tf_op jit(solution)/shard_map/ppermute | solution.py:323
  242.3 57.8 %collective-permute-start.48 = (bf16[256,768]{1,0:T(8,128)(2,1)S(1)}, bf16[256,768]{1,0:T(8,128)(2,1)}, u32[]{:S(2)}, u32[]{:S(2)}) collective-permute-start(bf16[256,768]{1,0:T(8,128)(2,1)S(1)} %get-tuple-element.92), channel_id=1, source_target_pairs={{0,16},{4,20},{8,24},{12,28},{16,0},{20,4},{24,8},{28,12},{1,17},{... | collective-permute-start | bytes 1179656 | tf_op jit(solution)/shard_map/ppermute | solution.py:323
  243.0 58.6 %collective-permute-start.49 = (bf16[256,768]{1,0:T(8,128)(2,1)S(1)}, bf16[256,768]{1,0:T(8,128)(2,1)}, u32[]{:S(2)}, u32[]{:S(2)}) collective-permute-start(bf16[256,768]{1,0:T(8,128)(2,1)S(1)} %get-tuple-element.92), channel_id=1, source_target_pairs={{0,8},{4,12},{8,0},{12,4},{16,24},{20,28},{24,16},{28,20},{1,9},{5... | collective-permute-start | bytes 1179656 | tf_op jit(solution)/shard_map/ppermute | solution.py:323
  262.5 240.7 %all-reduce.3.cloned.1.call-start = ((), (), s32[]{:S(2)}) async-start(), calls=%async_computation.2 | async-start | bytes 786432 | tf_op jit(solution)/shard_map/psum | solution.py:607
  266.5 40.0 %collective-permute-start.50 = (bf16[256,768]{1,0:T(8,128)(2,1)S(1)}, bf16[256,768]{1,0:T(8,128)(2,1)}, u32[]{:S(2)}, u32[]{:S(2)}) collective-permute-start(bf16[256,768]{1,0:T(8,128)(2,1)S(1)} %get-tuple-element.92), channel_id=1, source_target_pairs={{0,24},{4,28},{8,16},{12,20},{16,8},{20,12},{24,0},{28,4},{1,25},{... | collective-permute-start | bytes 1179656 | tf_op jit(solution)/shard_map/ppermute | solution.py:323
  268.0 39.8 %collective-permute-start.52 = (bf16[256,768]{1,0:T(8,128)(2,1)}, bf16[256,768]{1,0:T(8,128)(2,1)}, u32[]{:S(2)}, u32[]{:S(2)}) collective-permute-start(bf16[256,768]{1,0:T(8,128)(2,1)} %get-tuple-element.89), channel_id=1, source_target_pairs={{0,16},{4,20},{8,24},{12,28},{16,0},{20,4},{24,8},{28,12},{1,17},{... | collective-permute-start | bytes 1179656 | tf_op jit(solution)/shard_map/ppermute | solution.py:323
  269.3 39.1 %collective-permute-start.53 = (bf16[256,768]{1,0:T(8,128)(2,1)}, bf16[256,768]{1,0:T(8,128)(2,1)}, u32[]{:S(2)}, u32[]{:S(2)}) collective-permute-start(bf16[256,768]{1,0:T(8,128)(2,1)} %get-tuple-element.89), channel_id=1, source_target_pairs={{0,8},{4,12},{8,0},{12,4},{16,24},{20,28},{24,16},{28,20},{1,9},{5... | collective-permute-start | bytes 1179656 | tf_op jit(solution)/shard_map/ppermute | solution.py:323
  306.5 42.4 %collective-permute-start.36 = (bf16[4,128,768]{2,1,0:T(8,128)(2,1)}, bf16[4,128,768]{2,1,0:T(8,128)(2,1)S(1)}, u32[]{:S(2)}, u32[]{:S(2)}) collective-permute-start(bf16[4,128,768]{2,1,0:T(8,128)(2,1)} %bitcast.100), channel_id=1, source_target_pairs={{0,4},{4,0},{8,12},{12,8},{16,20},{20,16},{24,28},{28,24},{1,5},{5... | collective-permute-start | bytes 2359304 | tf_op jit(solution)/shard_map/ppermute | solution.py:323
  307.9 60.2 %collective-permute-start.51 = (bf16[1024,768]{1,0:T(8,128)(2,1)S(1)}, bf16[1024,768]{1,0:T(8,128)(2,1)S(1)}, u32[]{:S(2)}, u32[]{:S(2)}) collective-permute-start(bf16[1024,768]{1,0:T(8,128)(2,1)S(1)} %pad_maximum_fusion), channel_id=1, source_target_pairs={{0,4},{4,0},{8,12},{12,8},{16,20},{20,16},{24,28},{28,24},{1,5},{5... | collective-permute-start | bytes 4718600 | tf_op jit(solution)/shard_map/ppermute | solution.py:323
  344.7 27.5 %collective-permute-start.55 = (bf16[1024,768]{1,0:T(8,128)(2,1)S(1)}, bf16[1024,768]{1,0:T(8,128)(2,1)S(1)}, u32[]{:S(2)}, u32[]{:S(2)}) collective-permute-start(bf16[1024,768]{1,0:T(8,128)(2,1)S(1)} %pad_maximum_fusion.1), channel_id=1, source_target_pairs={{0,4},{4,0},{8,12},{12,8},{16,20},{20,16},{24,28},{28,24},{1,5},{5... | collective-permute-start | bytes 4718600 | tf_op jit(solution)/shard_map/ppermute | solution.py:323
  424.3 24.1 %collective-permute-start.69 = (bf16[4,96,768]{2,1,0:T(8,128)(2,1)}, bf16[4,96,768]{2,1,0:T(8,128)(2,1)}, u32[]{:S(2)}, u32[]{:S(2)}) collective-permute-start(bf16[4,96,768]{2,1,0:T(8,128)(2,1)} %pad_maximum_fusion.25), channel_id=1, source_target_pairs={{0,4},{4,0},{8,12},{12,8},{16,20},{20,16},{24,28},{28,24},{1,5},{5... | collective-permute-start | bytes 1769480 | tf_op jit(solution)/shard_map/ppermute | solution.py:323
  (161 other events, 1206.6 us)
Sparse Core Ops, SparseCore 0:
  262.6 33.5 reduce-scatter.1
  449.9 53.2 all-reduce.2
